TPU v7x, 32 devices: a whole 2x2x4 slice. The times are simulated.
32 devices in a mesh: tm: 4 (over z), space: 8 (over y, x, core).
Axes of the slice: x: 2, y: 2, z: 4, core: 2. Of those that a mesh axis runs over, the one named last changes fastest.
Arguments:
- tokens: bfloat16 [8192, 1024], P(('tm', 'space')), may hold values from -6 to 6
- latents: bfloat16 [512, 1024], replicated, may hold values from -300 to 300
- up_weight: bfloat16 [1024, 4096], P(None, 'tm'), may hold values from -0.1875 to 0.1875
- down_weight: bfloat16 [4096, 1024], P('tm'), may hold values from -0.09375 to 0.09375
Outputs:
- new_tokens: bfloat16 [8192, 1024], P(('tm', 'space'))
- new_latents: bfloat16 [512, 1024], P('space')
All inputs are finite; a program needn't handle non-finite values.
Results may differ from a plain program's by a relative error of at most 0.012.
The roundings to bfloat16 on the way count: a program that leaves them out, or rounds other values in their place, can miss the bound.
Values may be sent and summed in bfloat16 or wider, within the bound.
A program may use at most 64 MiB of HBM per device.

v0:
```python
import jax
import jax.numpy as jnp
from jax import lax
from jax.sharding import PartitionSpec as P

H = 16


epsilon = 1e-05
head_groups = 4


def layer_norm(values):
    center = values - jnp.mean(values, axis=-1, keepdims=True)
    spread = jnp.mean(center * center, axis=-1, keepdims=True)
    return center * lax.rsqrt(spread + epsilon)


def split_heads(matrix, head_count):
    row_count = matrix.shape[0]
    head_size = matrix.shape[1] // head_count
    return matrix.reshape(row_count, head_groups, head_count // head_groups, head_size).transpose(
        1, 2, 0, 3
    )


def per_head(weighted, factor):
    row_count = weighted.shape[0]
    return (weighted.reshape(row_count, factor.shape[1], -1) * factor[:, :, None]).reshape(
        row_count, weighted.shape[1]
    )


def read_partial(queries, keys_tok, tokens, head_count):
    score_scale = (queries.shape[1] // head_count) ** (-0.5)

    def read_one_group(operands):
        query_part, key_part, value_part = operands
        scores = (
            jnp.einsum("hld,htd->hlt", query_part, key_part, preferred_element_type=jnp.float32)
            * score_scale
        )
        row_peak = jnp.max(scores, axis=-1)
        weights = jnp.exp(scores - row_peak[..., None])
        row_total = jnp.sum(weights, axis=-1)
        weighted = jnp.einsum(
            "hlt,htd->lhd",
            weights.astype(jnp.bfloat16),
            value_part,
            preferred_element_type=jnp.float32,
        )
        return (row_peak, row_total, weighted)

    row_peak, row_total, weighted = lax.map(
        read_one_group,
        (
            split_heads(queries, head_count),
            split_heads(keys_tok, head_count),
            split_heads(tokens, head_count),
        ),
    )
    latent_count = queries.shape[0]
    row_peak = row_peak.reshape(head_count, latent_count).T
    row_total = row_total.reshape(head_count, latent_count).T
    weighted = weighted.transpose(1, 0, 2, 3).reshape(latent_count, queries.shape[1])
    return (row_peak, row_total, weighted)


def write_tokens(keys_tok, all_latents, tokens, head_count):
    score_scale = (all_latents.shape[1] // head_count) ** (-0.5)
    write_values = layer_norm(all_latents.astype(jnp.float32)).astype(jnp.bfloat16)

    def write_one_group(operands):
        query_part, key_part, value_part = operands
        scores = (
            jnp.einsum("htd,hld->htl", query_part, key_part, preferred_element_type=jnp.float32)
            * score_scale
        )
        weights = jnp.exp(scores - jnp.max(scores, axis=-1, keepdims=True))
        shares = (weights / jnp.sum(weights, axis=-1, keepdims=True)).astype(jnp.bfloat16)
        return jnp.einsum("htl,hld->thd", shares, value_part, preferred_element_type=jnp.float32)

    attended = lax.map(
        write_one_group,
        (
            split_heads(keys_tok, head_count),
            split_heads(all_latents, head_count),
            split_heads(write_values, head_count),
        ),
    )
    token_count = tokens.shape[0]
    attended = attended.transpose(1, 0, 2, 3).reshape(token_count, tokens.shape[1])
    return (tokens.astype(jnp.float32) + attended).astype(jnp.bfloat16)


def on_device(tokens, latents, up_weight, down_weight):
    head_count = H
    keys_tok = layer_norm(tokens.astype(jnp.float32)).astype(jnp.bfloat16)
    row_peak, row_total, weighted = read_partial(latents, keys_tok, tokens, head_count)
    owner_rows = latents.shape[0] // lax.axis_size("space")
    row_start = lax.axis_index("space") * owner_rows
    global_peak = lax.pmax(row_peak.astype(jnp.bfloat16), ("tm", "space")).astype(row_peak.dtype)
    factor = jnp.exp(row_peak - global_peak)
    scaled_total = row_total * factor
    scaled_weighted = per_head(weighted, factor)
    summed_total, summed_weighted = (
        lax.psum(scaled_total.astype(jnp.bfloat16), "tm").astype(jnp.float32),
        lax.psum(scaled_weighted.astype(jnp.bfloat16), "tm").astype(jnp.float32),
    )
    row_total, weighted = (
        lax.psum_scatter(
            summed_total.astype(jnp.bfloat16), "space", scatter_dimension=0, tiled=True
        ).astype(jnp.float32),
        lax.psum_scatter(
            summed_weighted.astype(jnp.bfloat16), "space", scatter_dimension=0, tiled=True
        ).astype(jnp.float32),
    )
    read_out = (weighted.reshape(owner_rows, head_count, -1) / row_total[:, :, None]).reshape(
        owner_rows, latents.shape[1]
    )
    own_latents = lax.dynamic_slice_in_dim(latents, row_start, owner_rows, 0).astype(jnp.float32)
    middle = own_latents + read_out
    normed = layer_norm(middle).astype(jnp.bfloat16)
    hidden_part = jax.nn.gelu(
        jnp.dot(normed, up_weight, preferred_element_type=jnp.float32), approximate=False
    ).astype(jnp.bfloat16)
    mlp_part = jnp.dot(hidden_part, down_weight, preferred_element_type=jnp.float32)
    new_latents = (
        middle + lax.psum(mlp_part.astype(jnp.bfloat16), "tm").astype(jnp.float32)
    ).astype(jnp.bfloat16)
    all_latents = lax.all_gather(new_latents, "space", axis=0, tiled=True)
    new_tokens = write_tokens(keys_tok, all_latents, tokens, head_count)
    return (new_tokens, new_latents)


def solution(mesh):
    in_specs = (P(("tm", "space"), None), P(), P(None, "tm"), P("tm", None))
    out_specs = (P(("tm", "space"), None), P("space", None))
    return jax.shard_map(
        on_device, mesh=mesh, in_specs=in_specs, out_specs=out_specs, check_vma=False
    )
```

profile of v0, /device:TPU:0, one launch (start us, length us, event | category | flops | bytes accessed | tf_op | source)
XLA Modules:
  0.0 288.4 jit_solution(9477675318781492862)
XLA Ops:
  7.3 1.4 copy.27
  9.2 2.3 copy.28
  11.4 12.6 %while.24 = (s32[]{:T(128)}, f32[4,4,512]{2,1,0:T(4,128)S(1)}, f32[4,4,512]{2,1,0:T(4,128)S(1)}, f32[4,512,4,64]{1,3,2,0:T(8,128)}, bf16[4,4,512,64]{2,3,1,0:T(8...) while((s32[]{:T(128)}, f32[4,4,512]{2,1,0:T(4,128)S(1)}, ...), condition=%wide.region_5.6_spmd, body=%wide.region_2.5_spmd.sunk | while | flops 138407936 | bytes 7407705 | solution.py:54
  11.4 1.5 multiply_reduce_fusion.4
  12.9 0.4 fusion.171
  13.3 1.3 fusion.172
  14.6 1.5 multiply_reduce_fusion.4
  16.4 1.3 fusion.172
  17.7 1.5 multiply_reduce_fusion.4
  19.2 0.4 fusion.171
  19.6 1.3 fusion.172
  20.9 1.5 multiply_reduce_fusion.4
  22.3 0.4 fusion.171
  22.7 1.3 fusion.172
  24.0 42.2 %pmax.7 = bf16[512,16]{0,1:T(8,128)(2,1)S(1)} all-reduce(bf16[512,16]{0,1:T(8,128)(2,1)S(1)} %bitcast_convert_fusion), channel_id=1, replica_groups=mesh['tm'=4,'space'=8] {'tm','space'}, use_global_device_ids=true, to_apply=%region_6.7 | all-reduce | flops 8192 | bytes 32768 | tf_op jit(solution)/shard_map/pmax | solution.py:102
  66.2 1.6 mul.75
  67.8 2.9 %copy.31 = f32[512,1024]{1,0:T(8,128)} copy(f32[512,1024]{0,1:T(8,128)} %bitcast.121) | data formatting | bytes 4194304 | tf_op jit(solution)/shard_map/mul | solution.py:29
  70.8 2.9 %copy.30 = f32[512,1024]{1,0:T(8,128)} copy(f32[512,1024]{0,1:T(8,128)} %bitcast.19) | data formatting | bytes 4194304 | tf_op jit(solution)/shard_map/reshape;reshape | solution.py:29
  73.7 3.5 %multiply_convert_fusion = bf16[512,1024]{1,0:T(8,128)(2,1)} fusion(f32[512,1024]{1,0:T(8,128)} %copy.30, f32[512,1024]{1,0:T(8,128)} %copy.31), kind=kLoop, calls=%fused_computation.49 | loop fusion | flops 1048576 | bytes 5242880 | tf_op jit(solution)/shard_map/convert_element_type | solution.py:108
  77.3 0.8 copy.37
  78.1 35.1 %reduce-scatter.5.cloned.1.call-done = bf16[64,1024]{1,0:T(8,128)(2,1)} async-done(((bf16[512,1024]{1,0:T(8,128)(2,1)}), bf16[64,1024]{1,0:T(8,128)(2,1)}) %reduce-scatter.5.cloned.1.call-update) | async-done | bytes 131088 | tf_op jit(solution)/shard_map/reduce_scatter | solution.py:114
  113.3 36.9 %reduce-scatter.7.cloned.1.call-done = bf16[64,16]{1,0:T(8,128)(2,1)} async-done(((bf16[512,16]{1,0:T(8,128)(2,1)}), bf16[64,16]{1,0:T(8,128)(2,1)}) %reduce-scatter.7.cloned.1.call-update) | async-done | bytes 2064
  150.2 0.8 copy.38
  151.0 11.7 %psum.25 = bf16[64,16]{0,1:T(8,128)(2,1)S(1)} all-reduce(bf16[64,16]{0,1:T(8,128)(2,1)S(1)} %copy.38), channel_id=1, replica_groups=mesh['tm'=4,'space'=8] {'tm'}, use_global_device_ids=true, to_apply=%region_9.10 | all-reduce | flops 1024 | bytes 4096 | tf_op jit(solution)/shard_map/psum | solution.py:107
  162.7 1.0 div.39
  163.7 1.9 div.40
  165.6 21.5 %all-reduce.5.cloned.1.call-done = bf16[64,1024]{1,0:T(8,128)(2,1)} async-done(((bf16[64,1024]{1,0:T(8,128)(2,1)}), bf16[64,1024]{1,0:T(8,128)(2,1)}) %all-reduce.5.cloned.1.call-update) | async-done | bytes 131088 | tf_op jit(solution)/shard_map/psum | solution.py:108
  187.1 1.2 fusion.148
  188.5 3.7 %convolution_convert_fusion = bf16[64,1024]{1,0:T(8,128)(2,1)} fusion(bf16[1024,1024]{1,0:T(8,128)(2,1)S(1)} %copy-done, bf16[1024,1024]{1,0:T(8,128)(2,1)} %param.10, f32[64,1024]{1,0:T(8,128)S(1)} %get-tuple-element.101, f32[64]{0:T(128)S(1)} %add_rsqrt_fusion.2, f32[64]{0:T(128)S(1)} %broadcast_multiply_fusion.2), kind=kOutput, calls=%fused_computation.55 | convolution fusion | flops 272957440 | bytes 4588032 | tf_op jit(solution)/shard_map/dot_general | solution.py:127
  192.3 34.2 %all-reduce.3.cloned.1.call-done = bf16[64,1024]{1,0:T(8,128)(2,1)} async-done(((bf16[64,1024]{1,0:T(8,128)(2,1)}), bf16[64,1024]{1,0:T(8,128)(2,1)}) %all-reduce.3.cloned.1.call-update) | async-done | bytes 131088 | tf_op jit(solution)/shard_map/psum | solution.py:129
  226.5 1.6 add_convert_fusion
  228.1 24.0 %all-gather.2.cloned.1.call-done = bf16[512,1024]{1,0:T(8,128)(2,1)} async-done(((bf16[64,1024]{1,0:T(8,128)(2,1)}), bf16[512,1024]{1,0:T(8,128)(2,1)}) %all-gather.2.cloned.1.call-update) | async-done | bytes 1048592 | tf_op jit(solution)/shard_map/all_gather | solution.py:131
  252.1 1.5 convert_reduce_fusion
  253.6 1.6 fusion.63
  255.3 1.3 fusion.64
  256.6 2.3 copy.33
  258.9 2.3 copy.34
  261.2 18.3 %while.25 = (s32[]{:T(128)}, f32[4,256,4,64]{1,3,2,0:T(8,128)}, bf16[4,4,512,64]{2,3,1,0:T(8,128)(2,1)}, bf16[4,4,256,64]{2,3,1,0:T(8,128)(2,1)S(1)}, bf16[4,4,512,64]{2,3,1,0:T(8,128)(2,1)}, /*index=5*/s32[]{:T(128)}) while((s32[]{:T(128)}, f32[4,256,4,64]{1,3,2,0:T(8,128)}, bf16[4,4,512,64]{2,3,1,0:T(8,128)(2,1)}, ...), condition=%wide.region_19.20_spmd, body=%wide.region_16.19_spmd.sunk | while | flops 204998656 | bytes 1322053 | solution.py:83
  261.2 1.8 fusion.179
  263.0 2.8 fusion.180
  265.8 1.8 fusion.179
  267.6 2.8 fusion.180
  270.4 1.8 fusion.179
  272.2 2.8 fusion.180
  275.0 1.8 fusion.179
  276.8 2.8 fusion.180
  279.6 1.3 fusion.69
  280.9 1.0 copy.35
  (38 shorter events, 1.6 us)
Async XLA Ops:
  7.2 181.4 %copy-start = (bf16[1024,1024]{1,0:T(8,128)(2,1)S(1)}, bf16[1024,1024]{1,0:T(8,128)(2,1)}, u32[]{:S(2)}) copy-start(bf16[1024,1024]{1,0:T(8,128)(2,1)} %param.11) | copy-start | bytes 6291460
  7.2 106.1 %reduce-scatter.5.cloned.1.call-start = ((), (), s32[]{:S(2)}) async-start(), calls=%async_computation.4 | async-start | bytes 1179648 | tf_op jit(solution)/shard_map/reduce_scatter | solution.py:114
  77.2 72.9 %reduce-scatter.7.cloned.1.call-start = ((), (), s32[]{:S(2)}) async-start(), calls=%async_computation.6 | async-start | bytes 147456
  78.1 109.0 %all-reduce.5.cloned.1.call-start = ((), (), s32[]{:S(2)}) async-start(), calls=%async_computation.5 | async-start | bytes 262144 | tf_op jit(solution)/shard_map/psum | solution.py:108
  113.3 113.2 %all-reduce.3.cloned.1.call-start = ((), (), s32[]{:S(2)}) async-start(), calls=%async_computation.2 | async-start | bytes 262144 | tf_op jit(solution)/shard_map/psum | solution.py:129
  192.2 59.9 %all-gather.2.cloned.1.call-start = ((), (), s32[]{:S(2)}) async-start(), calls=%async_computation.3 | async-start | bytes 1179648 | tf_op jit(solution)/shard_map/all_gather | solution.py:131
  252.1 3.2 %copy-start.1 = (bf16[512,1024]{1,0:T(8,128)(2,1)S(1)}, bf16[512,1024]{1,0:T(8,128)(2,1)}, u32[]{:S(2)}) copy-start(bf16[512,1024]{1,0:T(8,128)(2,1)} %all-gather.2.cloned.1.call-done) | copy-start | bytes 3145732
Sparse Core Ops, SparseCore 0:
  77.4 35.8 reduce-scatter.4
  116.8 33.3 reduce-scatter.6
  152.6 34.4 all-reduce.4
  192.4 34.0 all-reduce.2
  228.9 23.1 all-gather.1
where the time goes:
time: 289 us; the launch traced here: 288 us
  waiting for transfers between devices  152 us (53%)
  blocking collectives  53.8 us (19%)
  matrix products  33 us (11%)
  local copies, waits for them, and re-layouts  21.3 us (7%)
  other arithmetic  14.4 us (5%)
  between operations  13.9 us (5%)
    pmax x1, blocking collectives, on_device(): lax.pmax(row_peak.astype(jnp.bfloat16), ('tm', 'space'))  42.2 us
    unnamed x6, waiting for transfers between devices  36.9 us
    reduce_scatter x1, waiting for transfers between devices, on_device(): lax.psum_scatter(summed_weighted.astype(jnp.bfloat16), 'space', scatter_d...  35.1 us
    psum x1, waiting for transfers between devices, on_device(): lax.psum(mlp_part.astype(jnp.bfloat16), 'tm').astype(jnp.float32)  34.2 us
    all_gather x1, waiting for transfers between devices, on_device(): all_latents = lax.all_gather(new_latents, 'space', axis=0, tiled=True)  24 us
    psum x1, waiting for transfers between devices, on_device(): lax.psum(scaled_weighted.astype(jnp.bfloat16), 'tm').astype(jnp.float32)  21.5 us
    psum x1, blocking collectives, on_device(): lax.psum(scaled_total.astype(jnp.bfloat16), 'tm').astype(jnp.float32)  11.7 us
    dot_general x4, matrix products, write_one_group(): jnp.einsum('htl,hld->thd', shares, value_part, preferred_element_type=jnp...  11.1 us
  transfers between devices with their start and end apart: 5, of which 5 were waited for; matrix products, arithmetic and copies ran while one was open for 2% of the time, Pallas kernels for 0%

commit v1 on v0

v1 whole, which is shorter than its diff:
```python
import functools

import jax
import jax.numpy as jnp
from jax import lax
from jax.experimental import pallas as pl
from jax.experimental.pallas import tpu as pltpu
from jax.sharding import PartitionSpec as P

H = 16
EPSILON = 1e-05
LANES = 128
MESH = pl.DeviceIdType.MESH
F32 = jnp.float32
BF16 = jnp.bfloat16


def layer_norm(values):
    center = values - jnp.mean(values, axis=-1, keepdims=True)
    spread = jnp.mean(center * center, axis=-1, keepdims=True)
    return center * lax.rsqrt(spread + EPSILON)


def dot_nt(left, right):
    return lax.dot_general(
        left, right, (((1,), (1,)), ((), ())), preferred_element_type=F32
    )


def low_half(rows):
    return lax.broadcasted_iota(jnp.int32, (rows, LANES), 1) < LANES // 2


def head_parts(pair, fill):
    values = pair.astype(F32)
    low = low_half(pair.shape[0])
    return (
        jnp.where(low, values, fill).astype(BF16),
        jnp.where(low, fill, values).astype(BF16),
    )


def attend(queries, key_parts, value_parts):
    results, peaks = [], []
    for keys, values in zip(key_parts, value_parts):
        scores = dot_nt(queries, keys)
        peak = jnp.max(scores, axis=-1, keepdims=True)
        weights = jnp.exp(scores - peak).astype(BF16)
        results.append(jnp.dot(weights, values, preferred_element_type=F32))
        peaks.append(peak)
    low = low_half(queries.shape[0])
    weighted = jnp.where(low, results[0], results[1])
    total = pltpu.roll(jnp.where(low, results[1], results[0]), LANES // 2, 1)
    return weighted / total, jnp.where(low, peaks[0], peaks[1]), total


def pair_expansion(width):
    lane = lax.broadcasted_iota(jnp.int32, (LANES, width), 0)
    feature = lax.broadcasted_iota(jnp.int32, (LANES, width), 1)
    half = LANES // 2
    wanted = (feature % LANES) // half * half + feature // LANES
    return jnp.where(lane == wanted, 1.0, 0.0).astype(BF16)


def merge_shares(logs):
    sources, rows, _ = logs.shape
    peak = jnp.max(logs, axis=0)
    weights = jnp.exp(logs - peak[None])
    total = jnp.sum(weights, axis=0)
    shares = (weights / total[None]).reshape(sources * rows, LANES)
    high = shares.astype(BF16)
    low = (shares - high.astype(F32)).astype(BF16)
    return high, low, peak + jnp.log(total)


def kernel(
    n_tm, n_space, pieces,
    tokens_ref, latents_ref, up_hbm, down_hbm, new_tokens_ref, new_latents_ref,
    up_ref, down_ref, keys_ref, send_u, recv_u, send_l, recv_l, merged,
    z_send_u, z_recv_u, z_send_l, z_recv_l, read_out, mlp_send, mlp_recv,
    all_latents, write_values,
    weight_sem, su_send, su_recv, sl_send, sl_recv, zu_send, zu_recv, zl_send, zl_recv,
    ro_send, ro_recv, mlp_ssem, mlp_rsem, gz_send, gz_recv, gs_send, gs_recv,
):
    my_tm = lax.axis_index("tm")
    my_space = lax.axis_index("space")
    width = tokens_ref.shape[1]
    latent_count = latents_ref.shape[0]
    pairs = width // LANES
    rows = latent_count // n_space
    piece_rows = rows // pieces
    scale = (width // H) ** (-0.5)

    def around(count, mine):
        return [lax.rem(mine + k, count) for k in range(1, count)]

    space_peers = around(n_space, my_space)
    tm_peers = around(n_tm, my_tm)

    def copy(src, dst, send_sem, recv_sem, axis, peer):
        return pltpu.make_async_remote_copy(
            src_ref=src, dst_ref=dst, send_sem=send_sem, recv_sem=recv_sem,
            device_id={axis: peer}, device_id_type=MESH,
        )

    barrier = pltpu.get_barrier_semaphore()
    for peer in space_peers:
        pl.semaphore_signal(barrier, inc=1, device_id={"space": peer}, device_id_type=MESH)
    for peer in tm_peers:
        pl.semaphore_signal(barrier, inc=1, device_id={"tm": peer}, device_id_type=MESH)
    up_copy = pltpu.make_async_copy(up_hbm, up_ref, weight_sem.at[0])
    down_copy = pltpu.make_async_copy(down_hbm, down_ref, weight_sem.at[1])
    up_copy.start()
    down_copy.start()

    keys_ref[...] = (
        layer_norm(tokens_ref[...].astype(F32)).astype(BF16).astype(F32) * scale
    ).astype(BF16)
    pl.semaphore_wait(barrier, n_space + n_tm - 2)

    pair_lane = lax.broadcasted_iota(jnp.int32, (latent_count, LANES), 1) % (LANES // 2)

    def read_pair(i, logs):
        lanes = pl.ds(pl.multiple_of(i * LANES, LANES), LANES)
        share, peak, total = attend(
            latents_ref[:, lanes],
            head_parts(keys_ref[:, lanes], 0.0),
            head_parts(tokens_ref[:, lanes], 1.0),
        )
        send_u[:, i] = share.reshape(n_space, rows, LANES).astype(BF16)
        for peer in space_peers:
            copy(
                send_u.at[peer, i], recv_u.at[my_space, i],
                su_send.at[peer], su_recv.at[my_space], "space", peer,
            ).start()
        return jnp.where(pair_lane == i, peak + jnp.log(total), logs)

    logs = lax.fori_loop(0, pairs, read_pair, jnp.zeros((latent_count, LANES), F32))
    send_l[...] = logs.reshape(n_space, rows, LANES)
    for peer in space_peers:
        copy(
            send_l.at[peer], recv_l.at[my_space],
            sl_send.at[peer], sl_recv.at[my_space], "space", peer,
        ).start()
    recv_u[my_space] = send_u[my_space]
    recv_l[my_space] = send_l[my_space]
    expansion = pair_expansion(width)
    for peer in space_peers:
        copy(send_l.at[peer], recv_l.at[peer], sl_send.at[peer], sl_recv.at[peer], "space", peer).wait()
    high, low, merged_log = merge_shares(recv_l[...])
    for peer in space_peers:
        copy(send_u.at[peer], recv_u.at[peer], su_send.at[peer], su_recv.at[peer], "space", peer).wait()
    for i in range(pairs):
        lanes = slice(i * LANES, (i + 1) * LANES)
        factor = jnp.dot(high, expansion[:, lanes], preferred_element_type=F32)
        factor += jnp.dot(low, expansion[:, lanes], preferred_element_type=F32)
        merged[:, lanes] = jnp.sum(
            factor.reshape(n_space, rows, LANES) * recv_u[:, i].astype(F32), axis=0
        )

    mine = my_tm if pieces > 1 else 0
    if pieces > 1:
        z_send_u[...] = merged[...].reshape(pieces, piece_rows, width).astype(BF16)
        z_send_l[...] = merged_log.reshape(pieces, piece_rows, LANES)
    else:
        z_send_u[0] = merged[...].astype(BF16)
        z_send_l[0] = merged_log

    def slot(peer):
        return peer if pieces > 1 else 0

    for peer in tm_peers:
        copy(
            z_send_l.at[slot(peer)], z_recv_l.at[my_tm],
            zl_send.at[peer], zl_recv.at[my_tm], "tm", peer,
        ).start()
        copy(
            z_send_u.at[slot(peer)], z_recv_u.at[my_tm],
            zu_send.at[peer], zu_recv.at[my_tm], "tm", peer,
        ).start()
    z_recv_u[my_tm] = z_send_u[mine]
    z_recv_l[my_tm] = z_send_l[mine]
    for peer in tm_peers:
        copy(z_send_l.at[slot(peer)], z_recv_l.at[peer], zl_send.at[peer], zl_recv.at[peer], "tm", peer).wait()
        copy(z_send_u.at[slot(peer)], z_recv_u.at[peer], zu_send.at[peer], zu_recv.at[peer], "tm", peer).wait()
    high, low, _ = merge_shares(z_recv_l[...])
    factor = jnp.dot(high, expansion, preferred_element_type=F32)
    factor += jnp.dot(low, expansion, preferred_element_type=F32)
    piece = jnp.sum(
        factor.reshape(n_tm, piece_rows, width) * z_recv_u[...].astype(F32), axis=0
    )
    read_out[mine] = piece.astype(BF16)
    if pieces > 1:
        for peer in tm_peers:
            copy(
                read_out.at[my_tm], read_out.at[my_tm],
                ro_send.at[peer], ro_recv.at[my_tm], "tm", peer,
            ).start()
        for peer in tm_peers:
            copy(read_out.at[my_tm], read_out.at[peer], ro_send.at[peer], ro_recv.at[peer], "tm", peer).wait()

    own = pl.ds(pl.multiple_of(my_space * rows, rows), rows)
    merged[...] = latents_ref[own, :].astype(F32) + read_out[...].astype(F32).reshape(rows, width)
    normed = layer_norm(merged[...]).astype(BF16)
    up_copy.wait()
    hidden = jnp.dot(normed, up_ref[...], preferred_element_type=F32)
    hidden = (0.5 * hidden * (1.0 + lax.erf(hidden * (0.5 ** 0.5)))).astype(BF16)
    down_copy.wait()
    terms = jnp.dot(hidden, down_ref[...], preferred_element_type=F32)
    mlp_send[...] = terms.reshape(pieces, piece_rows, width).astype(BF16)
    for peer in tm_peers:
        copy(
            mlp_send.at[slot(peer)], mlp_recv.at[my_tm],
            mlp_ssem.at[peer], mlp_rsem.at[my_tm], "tm", peer,
        ).start()
    mlp_recv[my_tm] = mlp_send[mine]
    own_piece = pl.ds(pl.multiple_of(mine * piece_rows, piece_rows), piece_rows)
    for peer in tm_peers:
        copy(mlp_send.at[slot(peer)], mlp_recv.at[peer], mlp_ssem.at[peer], mlp_rsem.at[peer], "tm", peer).wait()
    all_latents[my_space, mine] = (
        merged[own_piece, :] + jnp.sum(mlp_recv[...].astype(F32), axis=0)
    ).astype(BF16)

    def spread(part):
        for peer in space_peers:
            copy(
                all_latents.at[my_space, part], all_latents.at[my_space, part],
                gs_send.at[peer, part], gs_recv.at[my_space, part], "space", peer,
            ).start()

    if pieces > 1:
        for peer in tm_peers:
            copy(
                all_latents.at[my_space, my_tm], all_latents.at[my_space, my_tm],
                gz_send.at[peer], gz_recv.at[my_tm], "tm", peer,
            ).start()
    spread(mine)
    if pieces > 1:
        for peer in tm_peers:
            copy(
                all_latents.at[my_space, my_tm], all_latents.at[my_space, peer],
                gz_send.at[peer], gz_recv.at[peer], "tm", peer,
            ).wait()
            spread(peer)
    new_latents_ref[...] = (
        all_latents[my_space].astype(F32).reshape(rows, width).astype(BF16)
    )
    for peer in space_peers:
        for part in range(pieces):
            copy(
                all_latents.at[my_space, part], all_latents.at[peer, part],
                gs_send.at[peer, part], gs_recv.at[peer, part], "space", peer,
            ).wait()

    def norm_block(s, carry):
        block = all_latents[s].astype(F32).reshape(rows, width)
        write_values[s] = layer_norm(block).astype(BF16)
        return carry

    lax.fori_loop(0, n_space, norm_block, 0)

    def write_pair(i, carry):
        lanes = pl.ds(pl.multiple_of(i * LANES, LANES), LANES)
        latent_pair = all_latents[:, :, :, lanes].astype(F32).reshape(latent_count, LANES)
        value_pair = write_values[:, :, lanes].astype(F32).reshape(latent_count, LANES)
        low = low_half(latent_count)
        key_parts = (
            jnp.where(low, latent_pair, 0.0).astype(BF16),
            jnp.where(low, 0.0, latent_pair).astype(BF16),
        )
        value_parts = (
            jnp.where(low, value_pair, 1.0).astype(BF16),
            jnp.where(low, 1.0, value_pair).astype(BF16),
        )
        share, _, _ = attend(keys_ref[:, lanes], key_parts, value_parts)
        new_tokens_ref[:, lanes] = (tokens_ref[:, lanes].astype(F32) + share).astype(BF16)
        return carry

    lax.fori_loop(0, pairs, write_pair, 0)


def on_device(n_tm, n_space, tokens, latents, up_weight, down_weight):
    token_count, width = tokens.shape
    latent_count = latents.shape[0]
    rows = latent_count // n_space
    pieces = n_tm if rows % (16 * n_tm) == 0 else 1
    piece_rows = rows // pieces
    pairs = width // LANES
    vmem = pl.BlockSpec(memory_space=pltpu.VMEM)
    anywhere = pl.BlockSpec(memory_space=pl.ANY)
    dma = pltpu.SemaphoreType.DMA
    scratch = [
        pltpu.VMEM(up_weight.shape, BF16),
        pltpu.VMEM(down_weight.shape, BF16),
        pltpu.VMEM((token_count, width), BF16),
        pltpu.VMEM((n_space, pairs, rows, LANES), BF16),
        pltpu.VMEM((n_space, pairs, rows, LANES), BF16),
        pltpu.VMEM((n_space, rows, LANES), F32),
        pltpu.VMEM((n_space, rows, LANES), F32),
        pltpu.VMEM((rows, width), F32),
        pltpu.VMEM((pieces, piece_rows, width), BF16),
        pltpu.VMEM((n_tm, piece_rows, width), BF16),
        pltpu.VMEM((pieces, piece_rows, LANES), F32),
        pltpu.VMEM((n_tm, piece_rows, LANES), F32),
        pltpu.VMEM((pieces, piece_rows, width), BF16),
        pltpu.VMEM((pieces, piece_rows, width), BF16),
        pltpu.VMEM((n_tm, piece_rows, width), BF16),
        pltpu.VMEM((n_space, pieces, piece_rows, width), BF16),
        pltpu.VMEM((n_space, rows, width), BF16),
        dma((2,)),
        dma((n_space,)), dma((n_space,)), dma((n_space,)), dma((n_space,)),
        dma((n_tm,)), dma((n_tm,)), dma((n_tm,)), dma((n_tm,)),
        dma((n_tm,)), dma((n_tm,)), dma((n_tm,)), dma((n_tm,)),
        dma((n_tm,)), dma((n_tm,)),
        dma((n_space, pieces)), dma((n_space, pieces)),
    ]
    return pl.pallas_call(
        functools.partial(kernel, n_tm, n_space, pieces),
        out_shape=(
            jax.ShapeDtypeStruct((token_count, width), BF16),
            jax.ShapeDtypeStruct((rows, width), BF16),
        ),
        in_specs=[vmem, vmem, anywhere, anywhere],
        out_specs=(vmem, vmem),
        scratch_shapes=scratch,
        compiler_params=pltpu.CompilerParams(
            collective_id=0, has_side_effects=True, vmem_limit_bytes=56 * 1024 * 1024
        ),
    )(tokens, latents, up_weight, down_weight)


def solution(mesh):
    n_tm, n_space = mesh.shape["tm"], mesh.shape["space"]
    in_specs = (P(("tm", "space"), None), P(), P(None, "tm"), P("tm", None))
    out_specs = (P(("tm", "space"), None), P("space", None))
    return jax.shard_map(
        functools.partial(on_device, n_tm, n_space),
        mesh=mesh, in_specs=in_specs, out_specs=out_specs, check_vma=False,
    )
```

time: 289 us -> 65.5 us (0.23)
  waiting for transfers between devices: 152 us -> 0 us
  Pallas kernels: 0 us -> 61.2 us
  blocking collectives: 53.8 us -> 0 us
  matrix products: 33 us -> 0 us
  local copies, waits for them, and re-layouts: 21.3 us -> 3.44 us
  other arithmetic: 14.4 us -> 0 us
  between operations: 13.9 us -> 0.64 us
    pallas_call x0 -> x1, Pallas kernels: none -> 61.2 us  [on_device(): pl.pallas_call(functools.partial(kernel, n_tm, n_space, pieces), out_shap...]
    psum x2 -> x0, waiting for transfers between devices: 55.7 us -> none  [the longest x1 34.2 us: on_device(): lax.psum(mlp_part.astype(jnp.bfloat16), 'tm').astype(jnp.float32)]
    pmax x1 -> x0, blocking collectives: 42.2 us -> none  [on_device(): lax.pmax(row_peak.astype(jnp.bfloat16), ('tm', 'space'))]
    unnamed x6 -> x0, waiting for transfers between devices: 36.9 us -> none
    reduce_scatter x1 -> x0, waiting for transfers between devices: 35.1 us -> none  [on_device(): lax.psum_scatter(summed_weighted.astype(jnp.bfloat16), 'space', scatter_d...]
    dot_general x13 -> x0, matrix products: 25.8 us -> none  [the longest x4 11.1 us: write_one_group(): jnp.einsum('htl,hld->thd', shares, value_part, preferred_element_type=jnp...]
    all_gather x1 -> x0, waiting for transfers between devices: 24 us -> none  [on_device(): all_latents = lax.all_gather(new_latents, 'space', axis=0, tiled=True)]
    psum x1 -> x0, blocking collectives: 11.7 us -> none  [on_device(): lax.psum(scaled_total.astype(jnp.bfloat16), 'tm').astype(jnp.float32)]
  transfers between devices with their start and end apart: 5 -> 0, of which waited for: 5 -> 0; matrix products, arithmetic and copies ran while one was open for 2% -> 0% of each run, Pallas kernels for 0% -> 0%
where the time goes in v1:
time: 65.5 us; the launch traced here: 65.3 us
  Pallas kernels  61.2 us (93%)
  local copies, waits for them, and re-layouts  3.44 us (5%)
    pallas_call x1, Pallas kernels, on_device(): pl.pallas_call(functools.partial(kernel, n_tm, n_space, pieces), out_shap...  61.2 us
    unnamed x2, local copies, waits for them, and re-layouts  3.44 us

profile of v1, /device:TPU:0, one launch (start us, length us, event | category | flops | bytes accessed | tf_op | source)
XLA Modules:
  0.0 65.3 jit_solution(15123518604656850094)
XLA Ops:
  0.6 61.2 %shard_map.59 = (bf16[256,1024]{1,0:T(8,128)(2,1)}, bf16[64,1024]{1,0:T(8,128)(2,1)}) custom-call(bf16[256,1024]{1,0:T(8,128)(2,1)} %tokens_ref.1, bf16[512,1024]{1,0:T(8,128)(2,1)} %latents_ref.1, bf16[1024,1024]{1,0:T(8,128)(2,1)} %up_hbm.1, bf16[1024,1024]{1,0:T(8,128)(2,1)} %down_hbm.1), custom_call_target="tpu_custom_call" | custom-call | tf_op jit(solution)/shard_map/pallas_call | solution.py:317
  61.8 1.9 %copy.8 = bf16[256,1024]{1,0:T(8,128)(2,1)} copy(bf16[256,1024]{1,0:T(8,128)(2,1)} %get-tuple-element.4) | data formatting | bytes 1048576
  63.7 1.6 %copy.9 = bf16[64,1024]{1,0:T(8,128)(2,1)} copy(bf16[64,1024]{1,0:T(8,128)(2,1)} %get-tuple-element.5) | data formatting | bytes 262144

commit v2 on v1

--- a/solution.py
+++ b/solution.py
@@ -81,6 +81,7 @@
     all_latents, write_values,
     weight_sem, su_send, su_recv, sl_send, sl_recv, zu_send, zu_recv, zl_send, zl_recv,
     ro_send, ro_recv, mlp_ssem, mlp_rsem, gz_send, gz_recv, gs_send, gs_recv,
+    gn_send,
 ):
     my_tm = lax.axis_index("tm")
     my_space = lax.axis_index("space")
@@ -96,6 +97,10 @@
 
     space_peers = around(n_space, my_space)
     tm_peers = around(n_tm, my_tm)
+    paired = n_space % 2 == 0
+    near_peers = [my_space + 1 - 2 * lax.rem(my_space, 2)] if paired else []
+    far_steps = range(2, n_space, 2) if paired else range(1, n_space)
+    far_peers = [lax.rem(my_space + step, n_space) for step in far_steps]
 
     def copy(src, dst, send_sem, recv_sem, axis, peer):
         return pltpu.make_async_remote_copy(
@@ -221,36 +226,65 @@
         merged[own_piece, :] + jnp.sum(mlp_recv[...].astype(F32), axis=0)
     ).astype(BF16)
 
+    def piece_copy(space, part, peer, send_sem, recv_sem, axis="space"):
+        block = all_latents.at[space, part]
+        return copy(block, block, send_sem, recv_sem, axis, peer)
+
     def spread(part):
-        for peer in space_peers:
-            copy(
-                all_latents.at[my_space, part], all_latents.at[my_space, part],
-                gs_send.at[peer, part], gs_recv.at[my_space, part], "space", peer,
-            ).start()
-
-    if pieces > 1:
-        for peer in tm_peers:
-            copy(
-                all_latents.at[my_space, my_tm], all_latents.at[my_space, my_tm],
-                gz_send.at[peer], gz_recv.at[my_tm], "tm", peer,
+        for peer in far_peers:
+            piece_copy(
+                my_space, part, peer, gs_send.at[peer, part], gs_recv.at[my_space, part]
+            ).start()
+        pass_on(my_space, part)
+
+    def pass_on(space, part):
+        for peer in near_peers:
+            piece_copy(
+                space, part, peer, gn_send.at[space, part], gs_recv.at[space, part]
+            ).start()
+
+    if pieces > 1:
+        for peer in tm_peers:
+            piece_copy(
+                my_space, my_tm, peer, gz_send.at[peer], gz_recv.at[my_tm], "tm"
             ).start()
     spread(mine)
-    if pieces > 1:
-        for peer in tm_peers:
-            copy(
-                all_latents.at[my_space, my_tm], all_latents.at[my_space, peer],
-                gz_send.at[peer], gz_recv.at[peer], "tm", peer,
-            ).wait()
+    parts = [mine]
+    if pieces > 1:
+        for peer in tm_peers:
+            piece_copy(
+                my_space, peer, peer, gz_send.at[peer], gz_recv.at[peer], "tm"
+            ).wait_recv()
             spread(peer)
+            parts.append(peer)
     new_latents_ref[...] = (
         all_latents[my_space].astype(F32).reshape(rows, width).astype(BF16)
     )
-    for peer in space_peers:
-        for part in range(pieces):
-            copy(
-                all_latents.at[my_space, part], all_latents.at[peer, part],
-                gs_send.at[peer, part], gs_recv.at[peer, part], "space", peer,
-            ).wait()
+    for part in parts:
+        for peer in far_peers:
+            piece_copy(
+                peer, part, peer, gs_send.at[peer, part], gs_recv.at[peer, part]
+            ).wait_recv()
+            pass_on(peer, part)
+    for part in parts:
+        for near in near_peers:
+            for space in [near] + [lax.rem(near + step, n_space) for step in far_steps]:
+                piece_copy(
+                    space, part, near, gn_send.at[my_space, part], gs_recv.at[space, part]
+                ).wait_recv()
+            for space in [my_space] + far_peers:
+                piece_copy(
+                    space, part, near, gn_send.at[space, part], gs_recv.at[space, part]
+                ).wait_send()
+        for peer in far_peers:
+            piece_copy(
+                my_space, part, peer, gs_send.at[peer, part], gs_recv.at[peer, part]
+            ).wait_send()
+    if pieces > 1:
+        for peer in tm_peers:
+            piece_copy(
+                my_space, my_tm, peer, gz_send.at[peer], gz_recv.at[peer], "tm"
+            ).wait_send()
 
     def norm_block(s, carry):
         block = all_latents[s].astype(F32).reshape(rows, width)
@@ -312,7 +346,7 @@
         dma((n_tm,)), dma((n_tm,)), dma((n_tm,)), dma((n_tm,)),
         dma((n_tm,)), dma((n_tm,)), dma((n_tm,)), dma((n_tm,)),
         dma((n_tm,)), dma((n_tm,)),
-        dma((n_space, pieces)), dma((n_space, pieces)),
+        dma((n_space, pieces)), dma((n_space, pieces)), dma((n_space, pieces)),
     ]
     return pl.pallas_call(
         functools.partial(kernel, n_tm, n_space, pieces),

time: 65.5 us -> 62.8 us (0.959)
  Pallas kernels: 61.2 us -> 58.6 us
    pallas_call x1, Pallas kernels: 61.2 us -> 58.6 us  [on_device(): pl.pallas_call(functools.partial(kernel, n_tm, n_space, pieces), out_shap...]
where the time goes in v2:
time: 62.8 us; the launch traced here: 62.6 us
  Pallas kernels  58.6 us (93%)
  local copies, waits for them, and re-layouts  3.44 us (5%)
  between operations  0.64 us (1%)
    pallas_call x1, Pallas kernels, on_device(): pl.pallas_call(functools.partial(kernel, n_tm, n_space, pieces), out_shap...  58.6 us
    unnamed x2, local copies, waits for them, and re-layouts  3.44 us

profile of v2, /device:TPU:0, one launch (start us, length us, event | category | flops | bytes accessed | tf_op | source)
XLA Modules:
  0.0 62.6 jit_solution(17237577195674861795)
XLA Ops:
  0.6 58.6 %shard_map.59 = (bf16[256,1024]{1,0:T(8,128)(2,1)}, bf16[64,1024]{1,0:T(8,128)(2,1)}) custom-call(bf16[256,1024]{1,0:T(8,128)(2,1)} %tokens_ref.1, bf16[512,1024]{1,0:T(8,128)(2,1)} %latents_ref.1, bf16[1024,1024]{1,0:T(8,128)(2,1)} %up_hbm.1, bf16[1024,1024]{1,0:T(8,128)(2,1)} %down_hbm.1), custom_call_target="tpu_custom_call" | custom-call | tf_op jit(solution)/shard_map/pallas_call | solution.py:351
  59.2 1.9 %copy.8 = bf16[256,1024]{1,0:T(8,128)(2,1)} copy(bf16[256,1024]{1,0:T(8,128)(2,1)} %get-tuple-element.4) | data formatting | bytes 1048576
  61.1 1.6 %copy.9 = bf16[64,1024]{1,0:T(8,128)(2,1)} copy(bf16[64,1024]{1,0:T(8,128)(2,1)} %get-tuple-element.5) | data formatting | bytes 262144

commit v3 on v2

--- a/solution.py
+++ b/solution.py
@@ -77,11 +77,12 @@
     n_tm, n_space, pieces,
     tokens_ref, latents_ref, up_hbm, down_hbm, new_tokens_ref, new_latents_ref,
     up_ref, down_ref, keys_ref, send_u, recv_u, send_l, recv_l, merged,
+    pair_tokens, pair_keys, half_u, half_l, pair_u, pair_l,
     z_send_u, z_recv_u, z_send_l, z_recv_l, read_out, mlp_send, mlp_recv,
     all_latents, write_values,
     weight_sem, su_send, su_recv, sl_send, sl_recv, zu_send, zu_recv, zl_send, zl_recv,
     ro_send, ro_recv, mlp_ssem, mlp_rsem, gz_send, gz_recv, gs_send, gs_recv,
-    gn_send,
+    gn_send, pt_send, pt_recv, sw_send, sw_recv,
 ):
     my_tm = lax.axis_index("tm")
     my_space = lax.axis_index("space")
@@ -95,11 +96,9 @@
     def around(count, mine):
         return [lax.rem(mine + k, count) for k in range(1, count)]
 
-    space_peers = around(n_space, my_space)
     tm_peers = around(n_tm, my_tm)
-    paired = n_space % 2 == 0
-    near_peers = [my_space + 1 - 2 * lax.rem(my_space, 2)] if paired else []
-    far_steps = range(2, n_space, 2) if paired else range(1, n_space)
+    near_peers = [my_space + 1 - 2 * lax.rem(my_space, 2)]
+    far_steps = range(2, n_space, 2)
     far_peers = [lax.rem(my_space + step, n_space) for step in far_steps]
 
     def copy(src, dst, send_sem, recv_sem, axis, peer):
@@ -109,7 +108,7 @@
         )
 
     barrier = pltpu.get_barrier_semaphore()
-    for peer in space_peers:
+    for peer in near_peers + far_peers:
         pl.semaphore_signal(barrier, inc=1, device_id={"space": peer}, device_id_type=MESH)
     for peer in tm_peers:
         pl.semaphore_signal(barrier, inc=1, device_id={"tm": peer}, device_id_type=MESH)
@@ -118,50 +117,97 @@
     up_copy.start()
     down_copy.start()
 
+    pl.semaphore_wait(barrier, len(near_peers) + len(far_peers) + n_tm - 1)
+
+    near = near_peers[0]
+    parity = lax.rem(my_space, 2)
+    chip = my_space // 2
+    token_count = tokens_ref.shape[0]
+    half_width = width // 2
+    half_pairs = pairs // 2
+    own_half = pl.ds(pl.multiple_of(parity * half_width, half_width), half_width)
+    near_half = pl.ds(pl.multiple_of((1 - parity) * half_width, half_width), half_width)
+    token_copy = copy(
+        tokens_ref.at[:, near_half], pair_tokens.at[1], pt_send.at[0], pt_recv.at[0], "space", near
+    )
+    key_copy = copy(
+        keys_ref.at[:, near_half], pair_keys.at[1], pt_send.at[1], pt_recv.at[1], "space", near
+    )
+    token_copy.start()
     keys_ref[...] = (
         layer_norm(tokens_ref[...].astype(F32)).astype(BF16).astype(F32) * scale
     ).astype(BF16)
-    pl.semaphore_wait(barrier, n_space + n_tm - 2)
-
-    pair_lane = lax.broadcasted_iota(jnp.int32, (latent_count, LANES), 1) % (LANES // 2)
+    key_copy.start()
+    pair_tokens[0] = tokens_ref[:, own_half]
+    pair_keys[0] = keys_ref[:, own_half]
+    expansion = pair_expansion(width)
+    lane = lax.broadcasted_iota(jnp.int32, (latent_count, LANES), 1) % (LANES // 2)
+    token_copy.wait()
+    key_copy.wait()
 
     def read_pair(i, logs):
         lanes = pl.ds(pl.multiple_of(i * LANES, LANES), LANES)
+        all_lanes = pl.ds(pl.multiple_of(parity * half_width + i * LANES, LANES), LANES)
         share, peak, total = attend(
-            latents_ref[:, lanes],
-            head_parts(keys_ref[:, lanes], 0.0),
-            head_parts(tokens_ref[:, lanes], 1.0),
+            latents_ref[:, all_lanes],
+            head_parts(pair_keys[:, :, lanes].reshape(2 * token_count, LANES), 0.0),
+            head_parts(pair_tokens[:, :, lanes].reshape(2 * token_count, LANES), 1.0),
         )
-        send_u[:, i] = share.reshape(n_space, rows, LANES).astype(BF16)
-        for peer in space_peers:
+        send_u[:, i] = share.reshape(n_space // 2, 2 * rows, LANES).astype(BF16)
+        for peer in far_peers:
             copy(
-                send_u.at[peer, i], recv_u.at[my_space, i],
+                send_u.at[peer // 2, i], recv_u.at[chip, i],
                 su_send.at[peer], su_recv.at[my_space], "space", peer,
             ).start()
-        return jnp.where(pair_lane == i, peak + jnp.log(total), logs)
-
-    logs = lax.fori_loop(0, pairs, read_pair, jnp.zeros((latent_count, LANES), F32))
-    send_l[...] = logs.reshape(n_space, rows, LANES)
-    for peer in space_peers:
+        return jnp.where(lane == i, peak + jnp.log(total), logs)
+
+    logs = lax.fori_loop(0, half_pairs, read_pair, jnp.zeros((latent_count, LANES), F32))
+    first = logs.astype(BF16).astype(F32)
+    second = (logs - first).astype(BF16).astype(F32)
+    third = logs - first - second
+    terms = jnp.where(
+        lane < 16, first, jnp.where(lane < 32, pltpu.roll(second, 16, 1), pltpu.roll(third, 32, 1))
+    )
+    send_l[...] = terms.reshape(n_space // 2, 2 * rows, LANES).astype(BF16)
+    for peer in far_peers:
         copy(
-            send_l.at[peer], recv_l.at[my_space],
+            send_l.at[peer // 2], recv_l.at[chip],
             sl_send.at[peer], sl_recv.at[my_space], "space", peer,
         ).start()
-    recv_u[my_space] = send_u[my_space]
-    recv_l[my_space] = send_l[my_space]
-    expansion = pair_expansion(width)
-    for peer in space_peers:
-        copy(send_l.at[peer], recv_l.at[peer], sl_send.at[peer], sl_recv.at[peer], "space", peer).wait()
-    high, low, merged_log = merge_shares(recv_l[...])
-    for peer in space_peers:
-        copy(send_u.at[peer], recv_u.at[peer], su_send.at[peer], su_recv.at[peer], "space", peer).wait()
-    for i in range(pairs):
+    recv_u[chip] = send_u[chip]
+    recv_l[chip] = send_l[chip]
+    for peer in far_peers:
+        copy(send_l.at[peer // 2], recv_l.at[peer // 2], sl_send.at[peer], sl_recv.at[peer], "space", peer).wait()
+    terms = recv_l[...].astype(F32).reshape(latent_count, LANES)
+    logs = terms + pltpu.roll(terms, LANES - 16, 1) + pltpu.roll(terms, LANES - 32, 1)
+    high, low, merged_log = merge_shares(logs.reshape(n_space // 2, 2 * rows, LANES))
+    half_l[...] = merged_log.reshape(2, rows, LANES)
+    for peer in far_peers:
+        copy(send_u.at[peer // 2], recv_u.at[peer // 2], su_send.at[peer], su_recv.at[peer], "space", peer).wait()
+    for i in range(half_pairs):
         lanes = slice(i * LANES, (i + 1) * LANES)
         factor = jnp.dot(high, expansion[:, lanes], preferred_element_type=F32)
         factor += jnp.dot(low, expansion[:, lanes], preferred_element_type=F32)
-        merged[:, lanes] = jnp.sum(
-            factor.reshape(n_space, rows, LANES) * recv_u[:, i].astype(F32), axis=0
-        )
+        half_u[:, :, lanes] = jnp.sum(
+            factor.reshape(n_space // 2, 2 * rows, LANES) * recv_u[:, i].astype(F32), axis=0
+        ).reshape(2, rows, LANES).astype(BF16)
+
+    swap_l = copy(
+        half_l.at[1 - parity], pair_l.at[parity], sw_send.at[0], sw_recv.at[0], "space", near
+    )
+    swap_u = copy(
+        half_u.at[1 - parity], pair_u.at[parity], sw_send.at[1], sw_recv.at[1], "space", near
+    )
+    swap_l.start()
+    swap_u.start()
+    pair_l[parity] = half_l[parity]
+    pair_u[parity] = half_u[parity]
+    copy(half_l.at[1 - parity], pair_l.at[1 - parity], sw_send.at[0], sw_recv.at[0], "space", near).wait()
+    copy(half_u.at[1 - parity], pair_u.at[1 - parity], sw_send.at[1], sw_recv.at[1], "space", near).wait()
+    row_lane = lax.broadcasted_iota(jnp.int32, (rows, LANES), 1) % (LANES // 2)
+    merged_log = jnp.where(row_lane < half_pairs, pair_l[0], pltpu.roll(pair_l[1], half_pairs, 1))
+    for half in range(2):
+        merged[:, half * half_width:(half + 1) * half_width] = pair_u[half].astype(F32)
 
     mine = my_tm if pieces > 1 else 0
     if pieces > 1:
@@ -327,11 +373,17 @@
         pltpu.VMEM(up_weight.shape, BF16),
         pltpu.VMEM(down_weight.shape, BF16),
         pltpu.VMEM((token_count, width), BF16),
-        pltpu.VMEM((n_space, pairs, rows, LANES), BF16),
-        pltpu.VMEM((n_space, pairs, rows, LANES), BF16),
-        pltpu.VMEM((n_space, rows, LANES), F32),
-        pltpu.VMEM((n_space, rows, LANES), F32),
+        pltpu.VMEM((n_space // 2, pairs // 2, 2 * rows, LANES), BF16),
+        pltpu.VMEM((n_space // 2, pairs // 2, 2 * rows, LANES), BF16),
+        pltpu.VMEM((n_space // 2, 2 * rows, LANES), BF16),
+        pltpu.VMEM((n_space // 2, 2 * rows, LANES), BF16),
         pltpu.VMEM((rows, width), F32),
+        pltpu.VMEM((2, token_count, width // 2), BF16),
+        pltpu.VMEM((2, token_count, width // 2), BF16),
+        pltpu.VMEM((2, rows, width // 2), BF16),
+        pltpu.VMEM((2, rows, LANES), F32),
+        pltpu.VMEM((2, rows, width // 2), BF16),
+        pltpu.VMEM((2, rows, LANES), F32),
         pltpu.VMEM((pieces, piece_rows, width), BF16),
         pltpu.VMEM((n_tm, piece_rows, width), BF16),
         pltpu.VMEM((pieces, piece_rows, LANES), F32),
@@ -347,6 +399,7 @@
         dma((n_tm,)), dma((n_tm,)), dma((n_tm,)), dma((n_tm,)),
         dma((n_tm,)), dma((n_tm,)),
         dma((n_space, pieces)), dma((n_space, pieces)), dma((n_space, pieces)),
+        dma((2,)), dma((2,)), dma((2,)), dma((2,)),
     ]
     return pl.pallas_call(
         functools.partial(kernel, n_tm, n_space, pieces),

time: 62.8 us -> 59.8 us (0.952)
  Pallas kernels: 58.6 us -> 55.5 us
    pallas_call x1, Pallas kernels: 58.6 us -> 55.5 us  [on_device(): pl.pallas_call(functools.partial(kernel, n_tm, n_space, pieces), out_shap...]
where the time goes in v3:
time: 59.8 us; the launch traced here: 59.6 us
  Pallas kernels  55.5 us (93%)
  local copies, waits for them, and re-layouts  3.44 us (6%)
  between operations  0.64 us (1%)
    pallas_call x1, Pallas kernels, on_device(): pl.pallas_call(functools.partial(kernel, n_tm, n_space, pieces), out_shap...  55.5 us
    unnamed x2, local copies, waits for them, and re-layouts  3.44 us

profile of v3, /device:TPU:0, one launch (start us, length us, event | category | flops | bytes accessed | tf_op | source)
XLA Modules:
  0.0 59.6 jit_solution(4185912191548016940)
XLA Ops:
  0.6 55.5 %shard_map.59 = (bf16[256,1024]{1,0:T(8,128)(2,1)}, bf16[64,1024]{1,0:T(8,128)(2,1)}) custom-call(bf16[256,1024]{1,0:T(8,128)(2,1)} %tokens_ref.1, bf16[512,1024]{1,0:T(8,128)(2,1)} %latents_ref.1, bf16[1024,1024]{1,0:T(8,128)(2,1)} %up_hbm.1, bf16[1024,1024]{1,0:T(8,128)(2,1)} %down_hbm.1), custom_call_target="tpu_custom_call" | custom-call | tf_op jit(solution)/shard_map/pallas_call | solution.py:404
  56.1 1.9 %copy.8 = bf16[256,1024]{1,0:T(8,128)(2,1)} copy(bf16[256,1024]{1,0:T(8,128)(2,1)} %get-tuple-element.4) | data formatting | bytes 1048576
  58.0 1.6 %copy.9 = bf16[64,1024]{1,0:T(8,128)(2,1)} copy(bf16[64,1024]{1,0:T(8,128)(2,1)} %get-tuple-element.5) | data formatting | bytes 262144

commit v4 on v3

--- a/solution.py
+++ b/solution.py
@@ -276,6 +276,10 @@
         block = all_latents.at[space, part]
         return copy(block, block, send_sem, recv_sem, axis, peer)
 
+    def norm_block(space):
+        block = all_latents[space].astype(F32).reshape(rows, width)
+        write_values[space] = layer_norm(block).astype(BF16)
+
     def spread(part):
         for peer in far_peers:
             piece_copy(
@@ -306,12 +310,15 @@
     new_latents_ref[...] = (
         all_latents[my_space].astype(F32).reshape(rows, width).astype(BF16)
     )
+    norm_block(my_space)
     for part in parts:
         for peer in far_peers:
             piece_copy(
                 peer, part, peer, gs_send.at[peer, part], gs_recv.at[peer, part]
             ).wait_recv()
             pass_on(peer, part)
+    for peer in far_peers:
+        norm_block(peer)
     for part in parts:
         for near in near_peers:
             for space in [near] + [lax.rem(near + step, n_space) for step in far_steps]:
@@ -332,12 +339,9 @@
                 my_space, my_tm, peer, gz_send.at[peer], gz_recv.at[peer], "tm"
             ).wait_send()
 
-    def norm_block(s, carry):
-        block = all_latents[s].astype(F32).reshape(rows, width)
-        write_values[s] = layer_norm(block).astype(BF16)
-        return carry
-
-    lax.fori_loop(0, n_space, norm_block, 0)
+    for near in near_peers:
+        for space in [near] + [lax.rem(near + step, n_space) for step in far_steps]:
+            norm_block(space)
 
     def write_pair(i, carry):
         lanes = pl.ds(pl.multiple_of(i * LANES, LANES), LANES)
@@ -356,7 +360,7 @@
         new_tokens_ref[:, lanes] = (tokens_ref[:, lanes].astype(F32) + share).astype(BF16)
         return carry
 
-    lax.fori_loop(0, pairs, write_pair, 0)
+    lax.fori_loop(0, pairs, write_pair, 0, unroll=4)
 
 
 def on_device(n_tm, n_space, tokens, latents, up_weight, down_weight):

time: 59.8 us -> 57.1 us (0.955)
  Pallas kernels: 55.5 us -> 52.8 us
    pallas_call x1, Pallas kernels: 55.5 us -> 52.8 us  [on_device(): pl.pallas_call(functools.partial(kernel, n_tm, n_space, pieces), out_shap...]
where the time goes in v4:
time: 57.1 us; the launch traced here: 56.9 us
  Pallas kernels  52.8 us (92%)
  local copies, waits for them, and re-layouts  3.44 us (6%)
  between operations  0.64 us (1%)
    pallas_call x1, Pallas kernels, on_device(): pl.pallas_call(functools.partial(kernel, n_tm, n_space, pieces), out_shap...  52.8 us
    unnamed x2, local copies, waits for them, and re-layouts  3.44 us

profile of v4, /device:TPU:0, one launch (start us, length us, event | category | flops | bytes accessed | tf_op | source)
XLA Modules:
  0.0 56.9 jit_solution(4484008124054860084)
XLA Ops:
  0.6 52.8 %shard_map.59 = (bf16[256,1024]{1,0:T(8,128)(2,1)}, bf16[64,1024]{1,0:T(8,128)(2,1)}) custom-call(bf16[256,1024]{1,0:T(8,128)(2,1)} %tokens_ref.1, bf16[512,1024]{1,0:T(8,128)(2,1)} %latents_ref.1, bf16[1024,1024]{1,0:T(8,128)(2,1)} %up_hbm.1, bf16[1024,1024]{1,0:T(8,128)(2,1)} %down_hbm.1), custom_call_target="tpu_custom_call" | custom-call | tf_op jit(solution)/shard_map/pallas_call | solution.py:408
  53.4 1.9 %copy.8 = bf16[256,1024]{1,0:T(8,128)(2,1)} copy(bf16[256,1024]{1,0:T(8,128)(2,1)} %get-tuple-element.4) | data formatting | bytes 1048576
  55.3 1.6 %copy.9 = bf16[64,1024]{1,0:T(8,128)(2,1)} copy(bf16[64,1024]{1,0:T(8,128)(2,1)} %get-tuple-element.5) | data formatting | bytes 262144

commit v5 on v4

--- a/solution.py
+++ b/solution.py
@@ -192,6 +192,20 @@
             factor.reshape(n_space // 2, 2 * rows, LANES) * recv_u[:, i].astype(F32), axis=0
         ).reshape(2, rows, LANES).astype(BF16)
 
+    mine = my_tm if pieces > 1 else 0
+
+    def slot(peer):
+        return peer if pieces > 1 else 0
+
+    def send_half(half, lanes):
+        block = pair_u[half].astype(F32).reshape(pieces, piece_rows, half_width)
+        z_send_u[:, :, lanes] = block.astype(BF16)
+        for peer in tm_peers:
+            copy(
+                z_send_u.at[slot(peer), :, lanes], z_recv_u.at[my_tm, :, lanes],
+                zu_send.at[peer], zu_recv.at[my_tm], "tm", peer,
+            ).start()
+
     swap_l = copy(
         half_l.at[1 - parity], pair_l.at[parity], sw_send.at[0], sw_recv.at[0], "space", near
     )
@@ -202,33 +216,19 @@
     swap_u.start()
     pair_l[parity] = half_l[parity]
     pair_u[parity] = half_u[parity]
+    send_half(parity, own_half)
     copy(half_l.at[1 - parity], pair_l.at[1 - parity], sw_send.at[0], sw_recv.at[0], "space", near).wait()
     copy(half_u.at[1 - parity], pair_u.at[1 - parity], sw_send.at[1], sw_recv.at[1], "space", near).wait()
     row_lane = lax.broadcasted_iota(jnp.int32, (rows, LANES), 1) % (LANES // 2)
     merged_log = jnp.where(row_lane < half_pairs, pair_l[0], pltpu.roll(pair_l[1], half_pairs, 1))
-    for half in range(2):
-        merged[:, half * half_width:(half + 1) * half_width] = pair_u[half].astype(F32)
-
-    mine = my_tm if pieces > 1 else 0
-    if pieces > 1:
-        z_send_u[...] = merged[...].reshape(pieces, piece_rows, width).astype(BF16)
-        z_send_l[...] = merged_log.reshape(pieces, piece_rows, LANES)
-    else:
-        z_send_u[0] = merged[...].astype(BF16)
-        z_send_l[0] = merged_log
-
-    def slot(peer):
-        return peer if pieces > 1 else 0
-
+
+    z_send_l[...] = merged_log.reshape(pieces, piece_rows, LANES)
     for peer in tm_peers:
         copy(
             z_send_l.at[slot(peer)], z_recv_l.at[my_tm],
             zl_send.at[peer], zl_recv.at[my_tm], "tm", peer,
         ).start()
-        copy(
-            z_send_u.at[slot(peer)], z_recv_u.at[my_tm],
-            zu_send.at[peer], zu_recv.at[my_tm], "tm", peer,
-        ).start()
+    send_half(1 - parity, near_half)
     z_recv_u[my_tm] = z_send_u[mine]
     z_recv_l[my_tm] = z_send_l[mine]
     for peer in tm_peers:

time: 57.1 us -> 56.1 us (0.982)
  Pallas kernels: 52.8 us -> 51.8 us
    pallas_call x1, Pallas kernels: 52.8 us -> 51.8 us  [on_device(): pl.pallas_call(functools.partial(kernel, n_tm, n_space, pieces), out_shap...]
where the time goes in v5:
time: 56.1 us; the launch traced here: 55.9 us
  Pallas kernels  51.8 us (92%)
  local copies, waits for them, and re-layouts  3.44 us (6%)
  between operations  0.64 us (1%)
    pallas_call x1, Pallas kernels, on_device(): pl.pallas_call(functools.partial(kernel, n_tm, n_space, pieces), out_shap...  51.8 us
    unnamed x2, local copies, waits for them, and re-layouts  3.44 us

profile of v5, /device:TPU:0, one launch (start us, length us, event | category | flops | bytes accessed | tf_op | source)
XLA Modules:
  0.0 55.9 jit_solution(3319114497560396391)
XLA Ops:
  0.6 51.8 %shard_map.59 = (bf16[256,1024]{1,0:T(8,128)(2,1)}, bf16[64,1024]{1,0:T(8,128)(2,1)}) custom-call(bf16[256,1024]{1,0:T(8,128)(2,1)} %tokens_ref.1, bf16[512,1024]{1,0:T(8,128)(2,1)} %latents_ref.1, bf16[1024,1024]{1,0:T(8,128)(2,1)} %up_hbm.1, bf16[1024,1024]{1,0:T(8,128)(2,1)} %down_hbm.1), custom_call_target="tpu_custom_call" | custom-call | tf_op jit(solution)/shard_map/pallas_call | solution.py:408
  52.4 1.9 %copy.8 = bf16[256,1024]{1,0:T(8,128)(2,1)} copy(bf16[256,1024]{1,0:T(8,128)(2,1)} %get-tuple-element.4) | data formatting | bytes 1048576
  54.3 1.6 %copy.9 = bf16[64,1024]{1,0:T(8,128)(2,1)} copy(bf16[64,1024]{1,0:T(8,128)(2,1)} %get-tuple-element.5) | data formatting | bytes 262144
